TPU v7x, 32 devices: a whole 2x2x4 slice. The times are simulated.
32 devices in a mesh: quad: 16 (over z, x, core), rows: 2 (over y).
Axes of the slice: x: 2, y: 2, z: 4, core: 2. Of those that a mesh axis runs over, the one named last changes fastest.
Arguments:
- solutions: bfloat16 [32, 2, 64, 16, 1280], P('quad', None, None, None, 'rows'), may hold values from -64 to 64
- angles: float32 [32], replicated, may hold values from -3.140625 to 3.140625
- qweights: float32 [2, 32], replicated, may hold values from -1 to 1
- neighbours: int32 [320, 8], P(('quad', 'rows')), may hold values from 0 to 319, as said below
- hblocks: bfloat16 [320, 64, 512], P(('quad', 'rows')), may hold values from -0.25 to 0.25
Outputs:
- h_moments: bfloat16 [1024, 20480], P(None, ('quad', 'rows'))
- ritz_matrices: float32 [512, 2, 2, 512], P('quad')
Inputs may be any that keep to these rules, and one draw needn't show every extreme that they name: neighbours[c, 0] = c, neighbours[c, 1] = min(c + 2, 319), neighbours[c, 2] = max(c - 2, 0); every entry lies within 2 of c.
All inputs are finite; a program needn't handle non-finite values.
Results may differ from a plain program's by a relative error of at most 0.0075.
Values may be sent and summed in bfloat16 or wider, within the bound.
A program may use at most 64 MiB of HBM per device.

v0:
```python
import jax
import jax.numpy as jnp
from jax import lax
from jax.sharding import PartitionSpec as P

LCOL = 64
QPTS = 32
KMOM = 8
NB = 8
HALO = 2


def extended(block, sides, width):
    for axis, dim in sides:
        count = lax.axis_size(axis)
        forward = [(i, i + 1) for i in range(count - 1)]
        backward = [(target, source) for source, target in forward]
        low = lax.ppermute(
            lax.slice_in_dim(block, block.shape[dim] - width, None, axis=dim), axis, forward
        )
        high = lax.ppermute(lax.slice_in_dim(block, 0, width, axis=dim), axis, backward)
        block = jnp.concatenate([low, block, high], axis=dim)
    return block


def moment_coefficients(angles, qweights):
    order = jnp.arange(KMOM, dtype=jnp.float32)[:, None]
    phase = order * angles[None, :]
    cosine = jnp.cos(phase)
    sine = jnp.sin(phase)
    real_coef = qweights[0][None, :] * cosine - qweights[1][None, :] * sine
    imag_coef = qweights[0][None, :] * sine + qweights[1][None, :] * cosine
    real_rows = jnp.stack([real_coef, -imag_coef], -1)
    imag_rows = jnp.stack([imag_coef, real_coef], -1)
    mixing = jnp.stack([real_rows, imag_rows], 0)
    return mixing.reshape(2 * KMOM, 2 * QPTS).astype(jnp.bfloat16)


def split_parts(product, half_cols, row_count):
    real_part = product[:row_count, :half_cols] + product[row_count:, half_cols:]
    imag_part = product[:row_count, half_cols:] - product[row_count:, :half_cols]
    return jnp.stack([real_part, imag_part], 1)


def gram_part(moments, applied, first_row, row_count, total_rows):
    half_cols = moments.shape[0] // 2
    chosen = jnp.concatenate(
        [
            lax.dynamic_slice_in_dim(moments, first_row, row_count, 0),
            lax.dynamic_slice_in_dim(moments, half_cols + first_row, row_count, 0),
        ],
        0,
    )
    contract = (((1,), (1,)), ((), ()))
    plain = lax.dot_general(chosen, moments, contract, preferred_element_type=jnp.float32)
    mixed = lax.dot_general(chosen, applied, contract, preferred_element_type=jnp.float32)
    ritz = jnp.stack(
        [split_parts(plain, half_cols, row_count), split_parts(mixed, half_cols, row_count)], 1
    )
    return ritz * (1.0 / total_rows)


def per_device(solutions, angles, qweights, neighbours, hblocks):
    groups = lax.axis_size("quad") * lax.axis_size("rows")
    rows_dev = solutions.shape[4]
    cells_dev = hblocks.shape[0]
    orbitals = hblocks.shape[1]
    half_cols = KMOM * LCOL
    mixing = moment_coefficients(angles, qweights)
    received = lax.all_to_all(solutions, "quad", split_axis=3, concat_axis=0, tiled=True)
    stacked = received.reshape(QPTS * 2, LCOL, received.shape[4])
    result = jnp.einsum("pq,qln->pln", mixing, stacked, preferred_element_type=jnp.float32)
    moments = result.reshape(2 * half_cols, received.shape[4]).astype(jnp.bfloat16)
    padded = extended(moments, ((("quad", "rows"), 1),), HALO * orbitals)
    first_cell = (
        lax.axis_index("quad") * lax.axis_size("rows") + lax.axis_index("rows")
    ) * cells_dev
    local_index = (neighbours - first_cell + HALO).reshape(-1)
    cellwise = padded.reshape(2 * half_cols, cells_dev + 2 * HALO, orbitals)
    nearby = jnp.take(cellwise, local_index, axis=1).reshape(
        2 * half_cols, cells_dev, NB * orbitals
    )
    applied = jnp.einsum("cam,xcm->xca", hblocks, nearby, preferred_element_type=jnp.float32)
    applied = applied.reshape(2 * half_cols, rows_dev).astype(jnp.bfloat16)
    total_rows = rows_dev * groups
    share_rows = half_cols // lax.axis_size("quad")
    summed = lax.psum(gram_part(moments, applied, 0, half_cols, total_rows), ("quad", "rows"))
    ritz_matrices = lax.dynamic_slice_in_dim(
        summed, lax.axis_index("quad") * share_rows, share_rows, 0
    )
    return (applied, ritz_matrices)


def solution(mesh):
    in_specs = (
        P("quad", None, None, None, "rows"),
        P(),
        P(),
        P(("quad", "rows"), None),
        P(("quad", "rows"), None, None),
    )
    out_specs = (P(None, ("quad", "rows")), P("quad", None, None, None))
    return jax.shard_map(
        per_device, mesh=mesh, in_specs=in_specs, out_specs=out_specs, check_vma=False
    )
```

profile of v0, /device:TPU:0, one launch (start us, length us, event | category | flops | bytes accessed | tf_op | source)
XLA Modules:
  0.0 333.4 jit_solution(11366127904357081607)
XLA Ops:
  7.2 0.0 copy-start
  7.2 6.2 %copy.34 = bf16[2,2,64,16,640]{4,2,1,0,3:T(8,128)(2,1)} copy(bf16[2,2,64,16,640]{4,3,2,1,0:T(8,128)(2,1)} %param.5) | data formatting | bytes 10485760 | tf_op args[0]
  13.3 0.0 copy-start.5
  13.3 0.0 copy-start.6
  13.3 0.0 copy-start.4
  13.3 7.5 %all-to-all-start = ((bf16[2,2,64,16,640]{4,2,1,0,3:T(8,128)(2,1)}), bf16[2,2,64,16,640]{4,2,1,0,3:T(8,128)(2,1)}, u32[]{:S(2)}, u32[]{:S(2)}) async-start(bf16[2,2,64,16,640]{4,2,1,0,3:T(8,128)(2,1)} %copy.34), calls=%async_computation | async-start | bytes 10485760 | tf_op jit(solution)/shard_map/all_to_all | solution.py:70
  20.9 0.0 all-reduce.2.cloned.1.call-start
  20.9 0.0 copy-done.5
  21.0 0.0 copy-done.6
  21.0 0.1 negate_convert_fusion
  21.0 0.1 copy.33
  21.2 0.1 convert_element_type.30
  21.3 0.0 copy-done.4
  21.3 0.1 copy.39
  21.4 0.1 reshape.334
  21.5 0.1 copy.32
  21.6 0.1 broadcast_in_dim.16
  21.6 0.1 broadcast_in_dim.17
  21.8 95.1 %all-to-all-done = bf16[2,2,64,16,640]{4,2,1,0,3:T(8,128)(2,1)} async-done(((bf16[2,2,64,16,640]{4,2,1,0,3:T(8,128)(2,1)}), bf16[2,2,64,16,640]{4,2,1,0,3:T(8,128)(2,1)}, u32[]{:S(2)}, u32[]{:S(2)}) %all-to-all-start) | async-done | bytes 5242912 | tf_op jit(solution)/shard_map/all_to_all | solution.py:70
  116.8 6.5 %fusion.6 = bf16[16,64,640]{2,0,1:T(8,128)(2,1)S(1)} fusion(bf16[64,64,640]{2,1,0:T(8,128)(2,1)} %bitcast.7, bf16[16,64]{0,1:T(8,128)(2,1)S(1)} %convert_element_type.30), kind=kOutput, calls=%fused_computation.11 | convolution fusion | flops 84541440 | bytes 6555648 | tf_op jit(solution)/shard_map/pq,qln->pln/dot_general | solution.py:72
  123.3 0.3 copy.37
  123.6 0.0 copy-start.1
  123.7 1.8 fusion.23
  125.5 3.4 %collective-permute-start = (bf16[1024,128]{1,0:T(8,128)(2,1)S(1)}, bf16[1024,128]{1,0:T(8,128)(2,1)S(1)}, u32[]{:S(2)}, u32[]{:S(2)}) collective-permute-start(bf16[1024,128]{1,0:T(8,128)(2,1)S(1)} %get-tuple-element.14), channel_id=1, source_target_pairs={{0,1},{1,2},{2,3},{3,4},{4,5},{5,6},{6,7},{7,8},{8,9},{9,10},{10,1... | collective-permute-start | bytes 786440 | tf_op jit(solution)/shard_map/ppermute | solution.py:18
  128.9 1.5 collective-permute-start.1
  130.4 1.5 fusion.15
  131.9 3.7 %collective-permute-done = bf16[1024,128]{1,0:T(8,128)(2,1)S(1)} collective-permute-done((bf16[1024,128]{1,0:T(8,128)(2,1)S(1)}, bf16[1024,128]{1,0:T(8,128)(2,1)S(1)}, u32[]{:S(2)}, u32[]{:S(2)}) %collective-permute-start) | collective-permute-done | bytes 262176 | tf_op jit(solution)/shard_map/ppermute | solution.py:18
  135.6 1.6 collective-permute-done.1
  137.2 0.0 copy-done.1
  137.2 1.4 pad_maximum_fusion
  138.6 2.9 copy.38
  141.5 6.3 %gather_fusion = bf16[80,1024,64]{1,2,0:T(8,128)(2,1)} fusion(bf16[1024,14,64]{0,2,1:T(8,128)(2,1)S(1)} %bitcast.45, s32[1024]{0:T(1024)S(1)} %pad_clamp_fusion), kind=kCustom, calls=%fused_computation | custom fusion | bytes 20971840 | tf_op jit(solution)/shard_map/jit(_take)/gather | solution.py:80
  147.8 0.0 copy-done
  147.8 0.0 copy-start.2
  147.8 5.5 %fusion.9 = bf16[10,1024,64]{1,2,0:T(8,128)(2,1)S(1)} fusion(bf16[10,64,512]{2,1,0:T(8,128)(2,1)S(1)} %copy-done, bf16[1024,10,512]{0,2,1:T(8,128)(2,1)} %bitcast.46, pred[10,512]{1,0:T(8,128)(4,1)S(1)} %broadcast_in_dim.17), kind=kOutput, calls=%fused_computation.12 | convolution fusion | flops 676986880 | bytes 12456960 | tf_op jit(solution)/shard_map/cam,xcm->xca/dot_general | solution.py:83
  153.4 0.0 copy-done.2
  153.4 1.8 fusion.24
  155.2 0.0 copy-start.3
  155.2 0.5 fusion.13
  155.7 0.7 copy-done.3
  156.4 0.4 maximum_bitcast_fusion
  156.9 2.7 maximum_multiply_fusion
  159.6 0.0 all-reduce.2.cloned.1.call-update
  159.6 1.4 copy.41
  161.1 163.6 %all-reduce.2.cloned.1.call-done = f32[512,2,2,512]{3,0,2,1:T(8,128)} async-done(((f32[512,2,2,512]{3,0,2,1:T(8,128)}), f32[512,2,2,512]{3,0,2,1:T(8,128)}) %all-reduce.2.cloned.1.call-update) | async-done | bytes 4194320 | tf_op jit(solution)/shard_map/psum | solution.py:87
  324.7 1.0 constant_dynamic-slice_fusion
  325.6 0.9 copy.42
  (8 shorter events, 0.1 us)
Async XLA Ops:
  7.2 140.7 %copy-start = (bf16[10,64,512]{2,1,0:T(8,128)(2,1)S(1)}, bf16[10,64,512]{2,1,0:T(8,128)(2,1)}, u32[]{:S(2)}) copy-start(bf16[10,64,512]{2,1,0:T(8,128)(2,1)} %param.9) | copy-start | bytes 1966084
  13.3 7.6 %copy-start.5 = (f32[2,32]{1,0:T(2,128)S(1)}, f32[2,32]{1,0:T(2,128)}, u32[]{:S(2)}) copy-start(f32[2,32]{1,0:T(2,128)} %param.7) | copy-start | bytes 772
  13.3 7.6 %copy-start.6 = (f32[32]{0:T(128)S(1)}, f32[32]{0:T(128)}, u32[]{:S(2)}) copy-start(f32[32]{0:T(128)} %param.6) | copy-start | bytes 388
  13.3 7.9 %copy-start.4 = (s32[10,8]{0,1:T(8,128)S(1)}, s32[10,8]{0,1:T(8,128)}, u32[]{:S(2)}) copy-start(s32[10,8]{0,1:T(8,128)} %param.8) | copy-start | bytes 964
  13.3 103.5 %all-to-all-start = ((bf16[2,2,64,16,640]{4,2,1,0,3:T(8,128)(2,1)}), bf16[2,2,64,16,640]{4,2,1,0,3:T(8,128)(2,1)}, u32[]{:S(2)}, u32[]{:S(2)}) async-start(bf16[2,2,64,16,640]{4,2,1,0,3:T(8,128)(2,1)} %copy.34), calls=%async_computation | async-start | bytes 10485760 | tf_op jit(solution)/shard_map/all_to_all | solution.py:70
  20.9 303.8 %all-reduce.2.cloned.1.call-start = ((), (), s32[]{:S(2)}) async-start(), calls=%async_computation.1 | async-start | bytes 8388608 | tf_op jit(solution)/shard_map/psum | solution.py:87
  123.6 13.6 %copy-start.1 = (bf16[16,64,640]{2,1,0:T(8,128)(2,1)}, bf16[16,64,640]{2,1,0:T(8,128)(2,1)S(1)}, u32[]{:S(2)}) copy-start(bf16[16,64,640]{2,1,0:T(8,128)(2,1)S(1)} %copy.37) | copy-start | bytes 3932164
  125.5 10.1 %collective-permute-start = (bf16[1024,128]{1,0:T(8,128)(2,1)S(1)}, bf16[1024,128]{1,0:T(8,128)(2,1)S(1)}, u32[]{:S(2)}, u32[]{:S(2)}) collective-permute-start(bf16[1024,128]{1,0:T(8,128)(2,1)S(1)} %get-tuple-element.14), channel_id=1, source_target_pairs={{0,1},{1,2},{2,3},{3,4},{4,5},{5,6},{6,7},{7,8},{8,9},{9,10},{10,1... | collective-permute-start | bytes 786440 | tf_op jit(solution)/shard_map/ppermute | solution.py:18
  128.9 8.3 %collective-permute-start.1 = (bf16[1024,128]{1,0:T(8,128)(2,1)S(1)}, bf16[1024,128]{1,0:T(8,128)(2,1)S(1)}, u32[]{:S(2)}, u32[]{:S(2)}) collective-permute-start(bf16[1024,128]{1,0:T(8,128)(2,1)S(1)} %get-tuple-element.15), channel_id=1, source_target_pairs={{1,0},{2,1},{3,2},{4,3},{5,4},{6,5},{7,6},{8,7},{9,8},{10,9},{11,1... | collective-permute-start | bytes 786440 | tf_op jit(solution)/shard_map/ppermute | solution.py:21
  147.8 5.6 %copy-start.2 = (bf16[16,64,640]{2,1,0:T(8,128)(2,1)S(1)}, bf16[16,64,640]{2,1,0:T(8,128)(2,1)}, u32[]{:S(2)}) copy-start(bf16[16,64,640]{2,1,0:T(8,128)(2,1)} %copy-done.1) | copy-start | bytes 3932164
  155.2 1.2 copy-start.3
Sparse Core Ops, SparseCore 0:
  159.7 164.8 all-reduce.1
where the time goes:
time: 334 us; the launch traced here: 333 us
  waiting for transfers between devices  264 us (79%)
  local copies, waits for them, and re-layouts  20.4 us (6%)
  matrix products  15.7 us (5%)
  between operations  14.2 us (4%)
  starting transfers between devices  12.5 us (4%)
  other arithmetic  6.65 us (2%)
    psum x1, waiting for transfers between devices, per_device(): lax.psum(gram_part(moments, applied, 0, half_cols, total_rows), ('quad',...  164 us
    all_to_all x1, waiting for transfers between devices, per_device(): lax.all_to_all(solutions, 'quad', split_axis=3, concat_axis=0, tiled=True)  95.1 us
    unnamed x17, local copies, waits for them, and re-layouts  9.26 us
    all_to_all x1, starting transfers between devices, per_device(): lax.all_to_all(solutions, 'quad', split_axis=3, concat_axis=0, tiled=True)  7.53 us
  transfers between devices with their start and end apart: 4, of which 4 were waited for; matrix products, arithmetic and copies ran while one was open for 1% of the time, Pallas kernels for 0%

commit v1 on v0

--- a/solution.py
+++ b/solution.py
@@ -8,6 +8,12 @@
 KMOM = 8
 NB = 8
 HALO = 2
+
+
+def process_the_samples(piece_in, bus_axis, ax_name):
+    for h in (bus_axis, ax_name):
+        piece_in = lax.psum(piece_in, h)
+    return piece_in
 
 
 def extended(block, sides, width):
@@ -84,7 +90,9 @@
     applied = applied.reshape(2 * half_cols, rows_dev).astype(jnp.bfloat16)
     total_rows = rows_dev * groups
     share_rows = half_cols // lax.axis_size("quad")
-    summed = lax.psum(gram_part(moments, applied, 0, half_cols, total_rows), ("quad", "rows"))
+    summed = process_the_samples(
+        gram_part(moments, applied, 0, half_cols, total_rows), "rows", "quad"
+    )
     ritz_matrices = lax.dynamic_slice_in_dim(
         summed, lax.axis_index("quad") * share_rows, share_rows, 0
     )

time: 334 us -> 416 us (1.25)
  waiting for transfers between devices: 264 us -> 346 us
    psum x1 -> x2, waiting for transfers between devices: 164 us -> 245 us  [process_the_samples(): piece_in = lax.psum(piece_in, h)]
  transfers between devices with their start and end apart: 4 -> 5, of which waited for: 4 -> 5; matrix products, arithmetic and copies ran while one was open for 1% -> 1% of each run, Pallas kernels for 0% -> 0%
where the time goes in v1:
time: 416 us; the launch traced here: 415 us
  waiting for transfers between devices  346 us (83%)
  local copies, waits for them, and re-layouts  20.4 us (5%)
  matrix products  15.7 us (4%)
  between operations  14.3 us (3%)
  starting transfers between devices  12.5 us (3%)
  other arithmetic  6.65 us (2%)
    psum x2, waiting for transfers between devices, process_the_samples(): piece_in = lax.psum(piece_in, h)  245 us
    all_to_all x1, waiting for transfers between devices, per_device(): lax.all_to_all(solutions, 'quad', split_axis=3, concat_axis=0, tiled=True)  95.1 us
    unnamed x17, local copies, waits for them, and re-layouts  9.26 us
  transfers between devices with their start and end apart: 5, of which 5 were waited for; matrix products, arithmetic and copies ran while one was open for 1% of the time, Pallas kernels for 0%

profile of v1, /device:TPU:0, one launch (start us, length us, event | category | flops | bytes accessed | tf_op | source)
XLA Modules:
  0.0 415.2 jit_solution(16583726541498872045)
XLA Ops:
  7.2 0.0 copy-start
  7.2 6.2 %copy.34 = bf16[2,2,64,16,640]{4,2,1,0,3:T(8,128)(2,1)} copy(bf16[2,2,64,16,640]{4,3,2,1,0:T(8,128)(2,1)} %param.5) | data formatting | bytes 10485760 | tf_op args[0]
  13.3 0.0 copy-start.5
  13.3 0.0 copy-start.6
  13.3 0.0 copy-start.4
  13.3 7.5 %all-to-all-start = ((bf16[2,2,64,16,640]{4,2,1,0,3:T(8,128)(2,1)}), bf16[2,2,64,16,640]{4,2,1,0,3:T(8,128)(2,1)}, u32[]{:S(2)}, u32[]{:S(2)}) async-start(bf16[2,2,64,16,640]{4,2,1,0,3:T(8,128)(2,1)} %copy.34), calls=%async_computation | async-start | bytes 10485760 | tf_op jit(solution)/shard_map/all_to_all | solution.py:76
  20.9 0.0 all-reduce.3.cloned.1.call-start
  20.9 0.0 copy-done.5
  21.0 0.0 copy-done.6
  21.0 0.1 negate_convert_fusion
  21.0 0.1 copy.33
  21.2 0.1 convert_element_type.30
  21.3 0.0 copy-done.4
  21.3 0.1 copy.39
  21.4 0.1 reshape.334
  21.5 0.1 copy.32
  21.6 0.1 broadcast_in_dim.16
  21.6 0.1 broadcast_in_dim.17
  21.8 95.1 %all-to-all-done = bf16[2,2,64,16,640]{4,2,1,0,3:T(8,128)(2,1)} async-done(((bf16[2,2,64,16,640]{4,2,1,0,3:T(8,128)(2,1)}), bf16[2,2,64,16,640]{4,2,1,0,3:T(8,128)(2,1)}, u32[]{:S(2)}, u32[]{:S(2)}) %all-to-all-start) | async-done | bytes 5242912 | tf_op jit(solution)/shard_map/all_to_all | solution.py:76
  116.8 6.5 %fusion.6 = bf16[16,64,640]{2,0,1:T(8,128)(2,1)S(1)} fusion(bf16[64,64,640]{2,1,0:T(8,128)(2,1)} %bitcast.7, bf16[16,64]{0,1:T(8,128)(2,1)S(1)} %convert_element_type.30), kind=kOutput, calls=%fused_computation.11 | convolution fusion | flops 84541440 | bytes 6555648 | tf_op jit(solution)/shard_map/pq,qln->pln/dot_general | solution.py:78
  123.3 0.3 copy.37
  123.6 0.0 copy-start.1
  123.7 1.8 fusion.23
  125.5 3.4 collective-permute-start
  128.9 1.5 collective-permute-start.1
  130.4 1.5 fusion.15
  131.9 3.7 collective-permute-done
  135.6 1.6 collective-permute-done.1
  137.2 0.0 copy-done.1
  137.2 1.4 pad_maximum_fusion
  138.6 2.9 copy.38
  141.5 6.3 %gather_fusion = bf16[80,1024,64]{1,2,0:T(8,128)(2,1)} fusion(bf16[1024,14,64]{0,2,1:T(8,128)(2,1)S(1)} %bitcast.45, s32[1024]{0:T(1024)S(1)} %pad_clamp_fusion), kind=kCustom, calls=%fused_computation | custom fusion | bytes 20971840 | tf_op jit(solution)/shard_map/jit(_take)/gather | solution.py:86
  147.8 0.0 copy-done
  147.8 0.0 copy-start.2
  147.8 5.5 %fusion.9 = bf16[10,1024,64]{1,2,0:T(8,128)(2,1)S(1)} fusion(bf16[10,64,512]{2,1,0:T(8,128)(2,1)S(1)} %copy-done, bf16[1024,10,512]{0,2,1:T(8,128)(2,1)} %bitcast.46, pred[10,512]{1,0:T(8,128)(4,1)S(1)} %broadcast_in_dim.17), kind=kOutput, calls=%fused_computation.12 | convolution fusion | flops 676986880 | bytes 12456960 | tf_op jit(solution)/shard_map/cam,xcm->xca/dot_general | solution.py:89
  153.4 0.0 copy-done.2
  153.4 1.8 fusion.24
  155.2 0.0 copy-start.3
  155.2 0.5 fusion.13
  155.7 0.7 copy-done.3
  156.4 0.4 maximum_bitcast_fusion
  156.9 2.7 maximum_multiply_fusion
  159.6 0.0 all-reduce.3.cloned.1.call-update
  159.6 0.0 all-reduce.5.cloned.1.call-start
  159.7 131.1 %all-reduce.3.cloned.1.call-done = f32[512,2,2,512]{3,0,2,1:T(8,128)} async-done(((f32[512,2,2,512]{3,0,2,1:T(8,128)}), f32[512,2,2,512]{3,0,2,1:T(8,128)}) %all-reduce.3.cloned.1.call-update) | async-done | bytes 4194320 | tf_op jit(solution)/shard_map/psum | solution.py:15
  290.8 0.0 all-reduce.5.cloned.1.call-update
  290.8 1.4 copy.41
  292.3 114.2 %all-reduce.5.cloned.1.call-done = f32[512,2,2,512]{3,0,2,1:T(8,128)} async-done(((f32[512,2,2,512]{3,0,2,1:T(8,128)}), f32[512,2,2,512]{3,0,2,1:T(8,128)}) %all-reduce.5.cloned.1.call-update) | async-done | bytes 4194320 | tf_op jit(solution)/shard_map/psum | solution.py:15
  406.4 1.0 constant_dynamic-slice_fusion
  407.4 0.9 copy.42
  (8 shorter events, 0.1 us)
Async XLA Ops:
  7.2 140.7 %copy-start = (bf16[10,64,512]{2,1,0:T(8,128)(2,1)S(1)}, bf16[10,64,512]{2,1,0:T(8,128)(2,1)}, u32[]{:S(2)}) copy-start(bf16[10,64,512]{2,1,0:T(8,128)(2,1)} %param.9) | copy-start | bytes 1966084
  13.3 7.6 %copy-start.5 = (f32[2,32]{1,0:T(2,128)S(1)}, f32[2,32]{1,0:T(2,128)}, u32[]{:S(2)}) copy-start(f32[2,32]{1,0:T(2,128)} %param.7) | copy-start | bytes 772
  13.3 7.6 %copy-start.6 = (f32[32]{0:T(128)S(1)}, f32[32]{0:T(128)}, u32[]{:S(2)}) copy-start(f32[32]{0:T(128)} %param.6) | copy-start | bytes 388
  13.3 7.9 %copy-start.4 = (s32[10,8]{0,1:T(8,128)S(1)}, s32[10,8]{0,1:T(8,128)}, u32[]{:S(2)}) copy-start(s32[10,8]{0,1:T(8,128)} %param.8) | copy-start | bytes 964
  13.3 103.5 %all-to-all-start = ((bf16[2,2,64,16,640]{4,2,1,0,3:T(8,128)(2,1)}), bf16[2,2,64,16,640]{4,2,1,0,3:T(8,128)(2,1)}, u32[]{:S(2)}, u32[]{:S(2)}) async-start(bf16[2,2,64,16,640]{4,2,1,0,3:T(8,128)(2,1)} %copy.34), calls=%async_computation | async-start | bytes 10485760 | tf_op jit(solution)/shard_map/all_to_all | solution.py:76
  20.9 269.9 %all-reduce.3.cloned.1.call-start = ((), (), s32[]{:S(2)}) async-start(), calls=%async_computation.1 | async-start | bytes 8388608 | tf_op jit(solution)/shard_map/psum | solution.py:15
  123.6 13.6 %copy-start.1 = (bf16[16,64,640]{2,1,0:T(8,128)(2,1)}, bf16[16,64,640]{2,1,0:T(8,128)(2,1)S(1)}, u32[]{:S(2)}) copy-start(bf16[16,64,640]{2,1,0:T(8,128)(2,1)S(1)} %copy.37) | copy-start | bytes 3932164
  125.5 10.1 %collective-permute-start = (bf16[1024,128]{1,0:T(8,128)(2,1)S(1)}, bf16[1024,128]{1,0:T(8,128)(2,1)S(1)}, u32[]{:S(2)}, u32[]{:S(2)}) collective-permute-start(bf16[1024,128]{1,0:T(8,128)(2,1)S(1)} %get-tuple-element.14), channel_id=1, source_target_pairs={{0,1},{1,2},{2,3},{3,4},{4,5},{5,6},{6,7},{7,8},{8,9},{9,10},{10,1... | collective-permute-start | bytes 786440 | tf_op jit(solution)/shard_map/ppermute | solution.py:24
  128.9 8.3 %collective-permute-start.1 = (bf16[1024,128]{1,0:T(8,128)(2,1)S(1)}, bf16[1024,128]{1,0:T(8,128)(2,1)S(1)}, u32[]{:S(2)}, u32[]{:S(2)}) collective-permute-start(bf16[1024,128]{1,0:T(8,128)(2,1)S(1)} %get-tuple-element.15), channel_id=1, source_target_pairs={{1,0},{2,1},{3,2},{4,3},{5,4},{6,5},{7,6},{8,7},{9,8},{10,9},{11,1... | collective-permute-start | bytes 786440 | tf_op jit(solution)/shard_map/ppermute | solution.py:27
  147.8 5.6 %copy-start.2 = (bf16[16,64,640]{2,1,0:T(8,128)(2,1)S(1)}, bf16[16,64,640]{2,1,0:T(8,128)(2,1)}, u32[]{:S(2)}) copy-start(bf16[16,64,640]{2,1,0:T(8,128)(2,1)} %copy-done.1) | copy-start | bytes 3932164
  155.2 1.2 copy-start.3
  159.6 246.8 %all-reduce.5.cloned.1.call-start = ((), (), s32[]{:S(2)}) async-start(), calls=%async_computation.2 | async-start | bytes 8388608 | tf_op jit(solution)/shard_map/psum | solution.py:15
Sparse Core Ops, SparseCore 0:
  159.7 131.0 all-reduce.2
  294.9 111.4 all-reduce.4
